TPU v7x, 256 devices: a whole 4x4x8 slice. The times are simulated.
256 devices in a mesh: chan: 64 (over x_hi, y, z), seg: 4 (over x_lo, core).
Axes of the slice: x: 4 (x_hi: 2, x_lo: 2; x = x_hi * 2 + x_lo), y: 4, z: 8, core: 2. Of those that a mesh axis runs over, the one named last changes fastest.
Arguments:
- spectra: bfloat16 [2, 256, 2048, 256], P(None, 'seg', 'chan'), may hold values from -6 to 6
- pair_bins: int32 [64, 64, 1], P('chan'), may hold values from 0 to 127; in each aligned block of 64 rows (0 to 63, 64 to 127, ..., all dimensions but the last counted through in order) at most 2 rows name the same one
Outputs:
- offset_gathers: float32 [128, 256], P('chan', 'seg')
Inputs may be any that keep to these rules, and one draw needn't show every extreme that they name: `pair_bins`: in the 64 rows of one source block no bin is named more than 2 times; every bin is named by some row.
All inputs are finite; a program needn't handle non-finite values.
Results may differ from a plain program's by a relative error of at most 0.0003.
Values may be sent and summed in bfloat16 or wider, within the bound.
A program may use at most 64 MiB of HBM per device.

v0:
```python
import functools
import math

import jax
import jax.numpy as jnp
import numpy as np
from jax import lax
from jax.experimental import pallas as pl
from jax.experimental.pallas import tpu as pltpu
from jax.sharding import PartitionSpec as P

LAGS = 256
NFFT = 1024
LOW_BIN = 16
BIN_WIDTH = 4
REACH = 3
BIN_DEV = 2

MESH = pl.DeviceIdType.MESH
RING = 8
ROWS = 8
SEGS = 4
BLOCK = 32
PANELS = 64
HALO = REACH
CHUNKS = 4
F32 = jnp.float32
BF16 = jnp.bfloat16


def lag_table(freq_count, lag_count):
    bin_index = np.arange(freq_count, dtype=np.int64) + LOW_BIN
    lag_index = np.arange(lag_count, dtype=np.int64) - lag_count // 2
    phase = bin_index[:, None] * lag_index[None, :] % NFFT
    theta = phase.astype(np.float64) * (2.0 * math.pi / NFFT)
    return np.concatenate([np.cos(theta), -np.sin(theta)], axis=0).astype(np.float32)


def split_two(value):
    high = value.astype(BF16)
    return high, (value - high.astype(F32)).astype(BF16)


def kernel(
    norm_factor, x_ref, pb_ref, table_ref, o_ref,
    gathered, sources, sums, totals, panels, bins_in, stage_out, stage_in, last_out, last_in,
    local_sem, x_send, x_recv, h_send, h_recv, b_send, b_recv, s_send, s_recv, l_send, l_recv,
):
    chan = lax.axis_index("chan")
    seg = lax.axis_index("seg")
    z = lax.rem(chan, RING)
    row = lax.div(chan, RING)
    base = chan - z
    mine = row * SEGS + seg
    width = RING // CHUNKS

    def ring_peer(d):
        return lax.rem(z + d, RING)

    next_row = lax.rem(row + 1, ROWS) * RING + z
    prev_row = lax.rem(row + ROWS - 1, ROWS) * RING + z

    barrier = pltpu.get_barrier_semaphore()
    for d in range(1, RING):
        pl.semaphore_signal(barrier, inc=1, device_id=(base + ring_peer(d), seg), device_id_type=MESH)
    pl.semaphore_signal(barrier, inc=1, device_id=(next_row, seg), device_id_type=MESH)
    pl.semaphore_signal(barrier, inc=1, device_id=(prev_row, seg), device_id_type=MESH)

    def greet(d, carry):
        other = lax.rem(mine + d, ROWS * SEGS)
        pl.semaphore_signal(
            barrier, inc=1,
            device_id=(lax.div(other, SEGS) * RING + z, lax.rem(other, SEGS)), device_id_type=MESH,
        )
        return carry

    lax.fori_loop(1, ROWS * SEGS, greet, 0)
    own = pltpu.make_async_copy(x_ref.at[:, pl.ds(z * RING, RING)], gathered.at[HALO + z], local_sem.at[0])
    own.start()
    own_bins = pltpu.make_async_copy(pb_ref, bins_in.at[z], local_sem.at[1])
    own_bins.start()
    pl.semaphore_wait(barrier, RING - 1 + 2 + ROWS * SEGS - 1)

    order = [4, 3, 5, 2, 6, 1, 7]

    def block_copy(chunk, d):
        to = ring_peer(d)
        return pltpu.make_async_remote_copy(
            src_ref=x_ref.at[:, pl.ds(to * RING + chunk * width, width)],
            dst_ref=gathered.at[HALO + z, :, pl.ds(chunk * width, width)],
            send_sem=x_send.at[chunk, d], recv_sem=x_recv.at[chunk, d],
            device_id=(base + to, seg), device_id_type=MESH,
        )

    def halo_copy(chunk):
        return pltpu.make_async_remote_copy(
            src_ref=gathered.at[pl.ds(RING, HALO), :, pl.ds(chunk * width, width)],
            dst_ref=gathered.at[pl.ds(0, HALO), :, pl.ds(chunk * width, width)],
            send_sem=h_send.at[chunk], recv_sem=h_recv.at[chunk],
            device_id=(next_row, seg), device_id_type=MESH,
        )

    def bins_copy(d):
        return pltpu.make_async_remote_copy(
            src_ref=pb_ref, dst_ref=bins_in.at[z],
            send_sem=b_send.at[d], recv_sem=b_recv.at[d],
            device_id=(base + ring_peer(d), seg), device_id_type=MESH,
        )

    for chunk in range(min(2, CHUNKS)):
        for d in order:
            block_copy(chunk, d).start()
    for d in order:
        bins_copy(d).start()

    def clear(n, carry):
        totals[n] = jnp.zeros(totals.shape[1:], F32)
        return carry

    lax.fori_loop(0, totals.shape[0], clear, 0)
    own.wait()
    own_bins.wait()

    def prepare(chunk, n, is_source):
        for w in range(width):
            for tile in range(2):
                lanes = pl.ds(tile * 128, 128)
                real = gathered[n, 0, chunk * width + w, :, lanes].astype(F32)
                imag = gathered[n, 1, chunk * width + w, :, lanes].astype(F32)
                if is_source:
                    sources[n - HALO, w, 0, tile] = real
                    sources[n - HALO, w, 1, tile] = imag
                    sources[n - HALO, w, 2, tile] = real - imag
                parts = []
                for part in (real, imag):
                    padded = jnp.concatenate([jnp.zeros((8, 128), F32), part], axis=0)
                    pairs = padded + pltpu.roll(padded, BLOCK + 8 - 1, 0)
                    parts.append((padded, pairs + pltpu.roll(pairs, BLOCK + 8 - 2, 0)))
                (real_pad, real_sum), (imag_pad, imag_sum) = parts
                odd_real = pltpu.roll(real_sum, BLOCK + 8 - 4, 0)
                odd_imag = pltpu.roll(imag_sum, BLOCK + 8 - 4, 0)
                sums[n, w, 0, 0, tile] = real_sum
                sums[n, w, 0, 1, tile] = imag_sum
                sums[n, w, 0, 2, tile] = real_sum + imag_sum
                sums[n, w, 1, 0, tile] = odd_real
                sums[n, w, 1, 1, tile] = odd_imag
                sums[n, w, 1, 2, tile] = odd_real + odd_imag
                if is_source:
                    other_real = real_sum - real_pad
                    other_imag = imag_sum - imag_pad
                    sums[n + RING, w, 0, 0, tile] = other_real
                    sums[n + RING, w, 0, 1, tile] = other_imag
                    sums[n + RING, w, 0, 2, tile] = other_real + other_imag

    def correlate(s, k):
        partner = HALO + s - k
        centre = jnp.where(k == 0, HALO + RING + s, partner)
        for tile in range(2):
            for parity in range(2):
                place = (s * (REACH + 1) + k) * 4 + tile * 2 + parity
                acc = [[totals[place, q * 3 + m] for m in range(3)] for q in range(8)]
                for w in range(width):
                    left = [[sources[s, w, m, tile, 8 * i:8 * i + 8, :] for m in range(3)] for i in range(4)]
                    for j in range(-1, 4):
                        at = slice(8 * j + 8, 8 * j + 16)
                        right = [sums[partner, w, parity, m, tile, at, :] for m in range(3)]
                        for i in range(4):
                            q = j - i + 4
                            if not 0 <= q < 8:
                                continue
                            used = right
                            if parity == 0 and q == 4:
                                used = [sums[centre, w, 0, m, tile, at, :] for m in range(3)]
                            for m in range(3):
                                acc[q][m] = acc[q][m] + left[i][m] * used[m]
                for q in range(8):
                    for m in range(3):
                        totals[place, q * 3 + m] = acc[q][m]

    def one_chunk(chunk, carry):
        for d in order:
            block_copy(chunk, d).wait_recv()
        halo_copy(chunk).start()
        for d in order:
            block_copy(chunk, d).wait_send()

        @pl.when(chunk + 2 < CHUNKS)
        def _():
            for d in order:
                block_copy(chunk + 2, d).start()

        def ready(n, c):
            prepare(chunk, n, True)
            return c

        lax.fori_loop(HALO, HALO + RING, ready, 0)

        def inner(n, c):
            correlate(lax.div(n, REACH + 1), lax.rem(n, REACH + 1))
            return c

        lax.fori_loop(REACH * (REACH + 1), RING * (REACH + 1), inner, 0)
        halo_copy(chunk).wait_recv()

        def ready_halo(n, c):
            prepare(chunk, n, False)
            return c

        lax.fori_loop(0, HALO, ready_halo, 0)
        lax.fori_loop(0, REACH * (REACH + 1), inner, 0)
        halo_copy(chunk).wait_send()
        return carry

    lax.fori_loop(0, CHUNKS, one_chunk, 0)

    def finish(n, carry):
        s = lax.div(n, REACH + 1)
        k = lax.rem(n, REACH + 1)
        present = jnp.where((row > 0) | (s >= k), 1.0, 0.0).astype(F32)
        for tile in range(2):
            for parity in range(2):
                place = n * 4 + tile * 2 + parity
                real, imag = [], []
                for q in range(8):
                    a, b, c = (totals[place, q * 3 + m] for m in range(3))
                    real.append(jnp.sum(a + b, axis=0, keepdims=True))
                    imag.append(jnp.sum(c - a + b, axis=0, keepdims=True))
                where = pl.ds(n * 16 + parity * 8, 8)
                panels[where, tile * 128:tile * 128 + 128] = jnp.concatenate(real, axis=0) * present
                panels[where, 256 + tile * 128:256 + tile * 128 + 128] = jnp.concatenate(imag, axis=0) * present
        return carry

    lax.fori_loop(0, RING * (REACH + 1), finish, 0)

    for d in order:
        bins_copy(d).wait()

    index = lax.broadcasted_iota(jnp.int32, (128, PANELS), 0)
    owner_z = lax.div(index, 16)
    bin_ids = 2 * (lax.rem(index, 8) * RING + owner_z) + lax.rem(lax.div(index, 8), 2)
    binned = jnp.zeros((128, 512), F32)
    for s in range(RING):
        hot = jnp.where(bin_ids == bins_in[s, :, 0:PANELS], 1.0, 0.0).astype(BF16)
        for part in split_two(panels[s * PANELS:(s + 1) * PANELS, :]):
            binned = binned + jnp.dot(hot, part, preferred_element_type=F32)
    high, low = split_two(binned)
    table_high, table_low = split_two(table_ref[...])
    lagged = (
        jnp.dot(high, table_high, preferred_element_type=F32)
        + jnp.dot(low, table_high, preferred_element_type=F32)
        + jnp.dot(high, table_low, preferred_element_type=F32)
    )
    stage_out[...] = lagged.reshape(RING, 16, LAGS)

    def stage_copy(d):
        to = ring_peer(d)
        return pltpu.make_async_remote_copy(
            src_ref=stage_out.at[to], dst_ref=stage_in.at[z],
            send_sem=s_send.at[d], recv_sem=s_recv.at[d],
            device_id=(base + to, seg), device_id_type=MESH,
        )

    for d in order:
        stage_copy(d).start()
    own_part = stage_out[z]
    for d in order:
        stage_copy(d).wait_recv()
    summed = own_part
    for d in range(1, RING):
        summed = summed + stage_in[ring_peer(d)]
    for g in range(SEGS):
        both = jnp.concatenate([summed[0:8, g * 64:g * 64 + 64], summed[8:16, g * 64:g * 64 + 64]], axis=1)
        for r in range(ROWS):
            last_out[r * SEGS + g] = both[r:r + 1, :]

    def last_copy(d):
        other = lax.rem(mine + d, ROWS * SEGS)
        return pltpu.make_async_remote_copy(
            src_ref=last_out.at[other], dst_ref=last_in.at[mine],
            send_sem=l_send.at[d], recv_sem=l_recv.at[d],
            device_id=(lax.div(other, SEGS) * RING + z, lax.rem(other, SEGS)), device_id_type=MESH,
        )

    def last_start(d, carry):
        last_copy(d).start()
        return carry

    def last_wait(d, carry):
        last_copy(d).wait_recv()
        return carry

    def last_sent(d, carry):
        last_copy(d).wait_send()
        return carry

    lax.fori_loop(1, ROWS * SEGS, last_start, 0)
    for d in order:
        stage_copy(d).wait_send()
    result = last_out[mine]
    lax.fori_loop(1, ROWS * SEGS, last_wait, 0)
    for d in range(1, ROWS * SEGS):
        result = result + last_in[lax.rem(mine + d, ROWS * SEGS)]
    result = result * norm_factor
    o_ref[0:1, :] = result[:, 0:64]
    o_ref[1:2, :] = result[:, 64:128]
    lax.fori_loop(1, ROWS * SEGS, last_sent, 0)


def on_device(spectra, pair_bins):
    window_count = spectra.shape[1]
    freq_count = spectra.shape[3]
    panel_count = pair_bins.shape[1]
    norm_factor = 1.0 / math.sqrt(
        window_count * SEGS * BLOCK * BIN_WIDTH * freq_count * panel_count / BIN_DEV
    )
    ids = pair_bins.reshape(REACH + 1, 8, 2).transpose(0, 2, 1).reshape(1, panel_count)
    ids = jnp.pad(ids, ((0, 0), (0, 128 - panel_count)))
    table = jnp.asarray(lag_table(freq_count, LAGS))
    width = RING // CHUNKS
    vmem = pl.BlockSpec(memory_space=pltpu.VMEM)
    dma = pltpu.SemaphoreType.DMA
    return pl.pallas_call(
        functools.partial(kernel, norm_factor),
        out_shape=jax.ShapeDtypeStruct((BIN_DEV, LAGS // SEGS), F32),
        in_specs=[pl.BlockSpec(memory_space=pl.ANY), vmem, vmem],
        out_specs=vmem,
        scratch_shapes=[
            pltpu.VMEM((HALO + RING, 2, RING, BLOCK, 256), BF16),
            pltpu.VMEM((RING, width, 3, 2, BLOCK, 128), F32),
            pltpu.VMEM((HALO + 2 * RING, width, 2, 3, 2, BLOCK + 8, 128), F32),
            pltpu.VMEM((RING * (REACH + 1) * 4, 24, 8, 128), F32),
            pltpu.VMEM((RING * PANELS, 512), F32),
            pltpu.VMEM((RING, 1, 128), jnp.int32),
            pltpu.VMEM((RING, 16, LAGS), F32),
            pltpu.VMEM((RING, 16, LAGS), F32),
            pltpu.VMEM((ROWS * SEGS, 1, 128), F32),
            pltpu.VMEM((ROWS * SEGS, 1, 128), F32),
            dma((2,)),
            dma((CHUNKS, RING)), dma((CHUNKS, RING)),
            dma((CHUNKS,)), dma((CHUNKS,)),
            dma((RING,)), dma((RING,)),
            dma((RING,)), dma((RING,)),
            dma((ROWS * SEGS,)), dma((ROWS * SEGS,)),
        ],
        compiler_params=pltpu.CompilerParams(
            collective_id=0, has_side_effects=True, vmem_limit_bytes=48 * 1024 * 1024
        ),
    )(spectra, ids, table)


def solution(mesh):
    in_specs = (P(None, "seg", "chan", None), P("chan", None, None))
    out_specs = P("chan", "seg")
    return jax.shard_map(
        on_device, mesh=mesh, in_specs=in_specs, out_specs=out_specs, check_vma=False
    )
```

profile of v0, /device:TPU:1, one launch (start us, length us, event | category | flops | bytes accessed | tf_op | source)
XLA Modules:
  0.0 86.8 jit_solution(3757451353647940969)
XLA Ops:
  0.0 0.5 broadcast.5
  0.5 1.3 %reduce.3 = s32[64]{0:T(128)S(1)} reduce(s32[1,64,1]{1,2,0:T(1,128)} %param.4, s32[]{:T(128)} %broadcast.5), dimensions={0,2}, to_apply=%param.4.reduce_sub_computation.3 | reduce | bytes 516 | tf_op args[1]
  1.8 0.1 reshape.6
  1.9 0.1 copy.5
  2.0 0.1 reshape.7
  2.1 0.0 copy-start
  2.1 1.6 %copy-done = bf16[2,64,32,256]{3,2,1,0:T(8,128)(2,1)S(1)} copy-done((bf16[2,64,32,256]{3,2,1,0:T(8,128)(2,1)S(1)}, bf16[2,64,32,256]{3,2,1,0:T(8,128)(2,1)}, u32[]{:S(2)}) %copy-start) | copy-done | bytes 2097176
  3.7 0.0 copy-start.1
  3.7 1.0 %copy-done.1 = f32[512,256]{1,0:T(8,128)S(1)} copy-done((f32[512,256]{1,0:T(8,128)S(1)}, f32[512,256]{1,0:T(8,128)}, u32[]{:S(2)}) %copy-start.1) | copy-done | bytes 524312
  4.8 81.4 %shard_map.37 = f32[2,64]{1,0:T(2,128)S(1)} custom-call(bf16[2,64,32,256]{3,2,1,0:T(8,128)(2,1)S(1)} %copy-done, s32[1,128]{1,0:T(1,128)S(1)} %pad.4.pb_ref, f32[512,256]{1,0:T(8,128)S(1)} %copy-done.1), custom_call_target="tpu_custom_call" | custom-call | tf_op jit(solution)/shard_map/pallas_call | solution.py:322
  86.2 0.6 copy.7
  (1 shorter events, 0.0 us)
Async XLA Ops:
  2.1 1.6 %copy-start = (bf16[2,64,32,256]{3,2,1,0:T(8,128)(2,1)S(1)}, bf16[2,64,32,256]{3,2,1,0:T(8,128)(2,1)}, u32[]{:S(2)}) copy-start(bf16[2,64,32,256]{3,2,1,0:T(8,128)(2,1)} %x_ref.1) | copy-start | bytes 6291460
  3.7 1.0 %copy-start.1 = (f32[512,256]{1,0:T(8,128)S(1)}, f32[512,256]{1,0:T(8,128)}, u32[]{:S(2)}) copy-start(f32[512,256]{1,0:T(8,128)} %constant.4.clone.table_ref) | copy-start | bytes 1572868
where the time goes:
time: 87 us; the launch traced here: 86.8 us
  Pallas kernels  81.4 us (94%)
  local copies, waits for them, and re-layouts  3.99 us (5%)
  other arithmetic  1.32 us (2%)
    pallas_call x1, Pallas kernels, on_device(): pl.pallas_call(functools.partial(kernel, norm_factor), out_shape=jax.Shap...  81.4 us
    unnamed x6, local copies, waits for them, and re-layouts  3.71 us

commit v1 on v0

v1 whole, which is shorter than its diff:
```python
import functools
import math

import jax
import jax.numpy as jnp
import numpy as np
from jax import lax
from jax.experimental import pallas as pl
from jax.experimental.pallas import tpu as pltpu
from jax.sharding import PartitionSpec as P

LAGS = 256
NFFT = 1024
LOW_BIN = 16
BIN_WIDTH = 4
REACH = 3
BIN_DEV = 2

MESH = pl.DeviceIdType.MESH
RING = 8
ROWS = 8
COLS = 4
SEGS = 4
SIDES = 2 * SEGS
BLOCK = 32
PANELS = 64
HALO = REACH
CHUNKS = 8
WIDTH = RING // CHUNKS
AHEAD = 2
EARLY = 1
F32 = jnp.float32
BF16 = jnp.bfloat16


def lag_table(freq_count, lag_count):
    bin_index = np.arange(freq_count, dtype=np.int64) + LOW_BIN
    lag_index = np.arange(lag_count, dtype=np.int64) - lag_count // 2
    phase = bin_index[:, None] * lag_index[None, :] % NFFT
    theta = phase.astype(np.float64) * (2.0 * math.pi / NFFT)
    return np.concatenate([np.cos(theta), -np.sin(theta)], axis=0).astype(np.float32)


def split_two(value):
    high = value.astype(BF16)
    return high, (value - high.astype(F32)).astype(BF16)


def fold(values):
    row = lax.broadcasted_iota(jnp.int32, (8, 128), 0)
    upper = row >= 4
    fours = []
    for q in range(4):
        a, b = values[q], values[q + 4]
        fours.append(jnp.where(upper, b, a) + pltpu.roll(jnp.where(upper, a, b), 4, 0))
    upper = lax.rem(row, 4) >= 2
    twos = []
    for q in range(2):
        a, b = fours[q], fours[q + 2]
        twos.append(jnp.where(upper, b + pltpu.roll(b, 2, 0), a + pltpu.roll(a, 6, 0)))
    upper = lax.rem(row, 2) >= 1
    a, b = twos
    return jnp.where(upper, b + pltpu.roll(b, 1, 0), a + pltpu.roll(a, 7, 0))


def kernel(
    norm_factor, x_ref, pb_ref, table_in, o_ref,
    gathered, sources, sums, totals, panels, bins_in, table, a_out, a_in, b_out, b_in, c_out, c_in,
    local_sem, x_send, x_recv, h_send, h_recv, p_send, p_recv, a_send, a_recv, b_send, b_recv, c_send, c_recv,
):
    chan = lax.axis_index("chan")
    seg = lax.axis_index("seg")
    z = lax.rem(chan, RING)
    row = lax.div(chan, RING)
    y = lax.rem(row, COLS)
    upper = lax.div(row, COLS)
    base = chan - z
    side = upper * SEGS + seg

    def ring_peer(d):
        return lax.rem(z + d, RING)

    def y_peer(d):
        return lax.rem(y + d, COLS)

    def side_peer(d):
        return lax.rem(side + d, SIDES)

    def side_device(other):
        return ((lax.div(other, SEGS) * COLS + y) * RING + z, lax.rem(other, SEGS))

    def y_device(other):
        return ((upper * COLS + other) * RING + z, seg)

    next_row = (lax.rem(row + 1, ROWS) * RING + z, seg)
    prev_row = (lax.rem(row + ROWS - 1, ROWS) * RING + z, seg)
    has_next = row < ROWS - 1
    has_prev = row > 0

    barrier = pltpu.get_barrier_semaphore()

    def greet(device):
        pl.semaphore_signal(barrier, inc=1, device_id=device, device_id_type=MESH)

    for d in range(1, RING):
        greet((base + ring_peer(d), seg))
    greet(next_row)
    greet(prev_row)
    for d in range(1, COLS):
        greet(y_device(y_peer(d)))
    for d in range(1, SIDES):
        greet(side_device(side_peer(d)))

    own = pltpu.make_async_copy(x_ref.at[:, pl.ds(z * RING, RING)], gathered.at[HALO + z], local_sem.at[0])
    own.start()
    own_bins = pltpu.make_async_copy(pb_ref.at[0], bins_in.at[z], local_sem.at[1])
    own_bins.start()
    own_table = pltpu.make_async_copy(table_in, table, local_sem.at[2])
    own_table.start()
    pl.semaphore_wait(barrier, RING - 1 + 2 + COLS - 1 + SIDES - 1)

    order = [4, 3, 5, 2, 6, 1, 7]

    def block_copy(chunk, d):
        to = ring_peer(d)
        return pltpu.make_async_remote_copy(
            src_ref=x_ref.at[:, pl.ds(to * RING + chunk * WIDTH, WIDTH)],
            dst_ref=gathered.at[HALO + z, :, pl.ds(chunk * WIDTH, WIDTH)],
            send_sem=x_send.at[chunk, d], recv_sem=x_recv.at[chunk, z],
            device_id=(base + to, seg), device_id_type=MESH,
        )

    def block_arrival(chunk, source):
        return pltpu.make_async_remote_copy(
            src_ref=x_ref.at[:, pl.ds(chunk * WIDTH, WIDTH)],
            dst_ref=gathered.at[HALO + source, :, pl.ds(chunk * WIDTH, WIDTH)],
            send_sem=x_send.at[chunk, 0], recv_sem=x_recv.at[chunk, source],
            device_id=(base + ring_peer(1), seg), device_id_type=MESH,
        )

    def halo_copy(chunk):
        return pltpu.make_async_remote_copy(
            src_ref=gathered.at[pl.ds(RING, HALO), :, pl.ds(chunk * WIDTH, WIDTH)],
            dst_ref=gathered.at[pl.ds(0, HALO), :, pl.ds(chunk * WIDTH, WIDTH)],
            send_sem=h_send.at[chunk], recv_sem=h_recv.at[chunk],
            device_id=next_row, device_id_type=MESH,
        )

    def bins_copy(d):
        return pltpu.make_async_remote_copy(
            src_ref=pb_ref.at[0], dst_ref=bins_in.at[z],
            send_sem=p_send.at[d], recv_sem=p_recv.at[d],
            device_id=(base + ring_peer(d), seg), device_id_type=MESH,
        )

    def send_chunk(chunk):
        for d in order:
            block_copy(chunk, d).start()

    first_sent = z >= RING - HALO
    for chunk in range(AHEAD):
        send_chunk(chunk)

    @pl.when(first_sent)
    def _():
        for chunk in range(AHEAD, AHEAD + EARLY):
            send_chunk(chunk)

    for d in order:
        bins_copy(d).start()

    def clear(n, carry):
        totals[n] = jnp.zeros(totals.shape[1:], F32)
        return carry

    lax.fori_loop(0, totals.shape[0], clear, 0)

    @pl.when(jnp.logical_not(has_prev))
    def _():
        gathered[0:HALO] = jnp.zeros((HALO,) + gathered.shape[1:], BF16)

    own.wait()

    def prepare(chunk, n, is_source):
        for w in range(WIDTH):
            for tile in range(2):
                lanes = pl.ds(tile * 128, 128)
                real = gathered[n, 0, chunk * WIDTH + w, :, lanes].astype(F32)
                imag = gathered[n, 1, chunk * WIDTH + w, :, lanes].astype(F32)
                if is_source:
                    sources[n - HALO, w, 0, tile] = real
                    sources[n - HALO, w, 1, tile] = imag
                    sources[n - HALO, w, 2, tile] = real - imag
                parts = []
                for part in (real, imag):
                    padded = jnp.concatenate([jnp.zeros((8, 128), F32), part], axis=0)
                    pairs = padded + pltpu.roll(padded, BLOCK + 8 - 1, 0)
                    parts.append((padded, pairs + pltpu.roll(pairs, BLOCK + 8 - 2, 0)))
                (real_pad, real_sum), (imag_pad, imag_sum) = parts
                odd_real = pltpu.roll(real_sum, BLOCK + 8 - 4, 0)
                odd_imag = pltpu.roll(imag_sum, BLOCK + 8 - 4, 0)
                sums[n, w, 0, 0, tile] = real_sum
                sums[n, w, 0, 1, tile] = imag_sum
                sums[n, w, 0, 2, tile] = real_sum + imag_sum
                sums[n, w, 1, 0, tile] = odd_real
                sums[n, w, 1, 1, tile] = odd_imag
                sums[n, w, 1, 2, tile] = odd_real + odd_imag
                if is_source:
                    other_real = real_sum - real_pad
                    other_imag = imag_sum - imag_pad
                    sums[n + RING, w, 0, 0, tile] = other_real
                    sums[n + RING, w, 0, 1, tile] = other_imag
                    sums[n + RING, w, 0, 2, tile] = other_real + other_imag

    def correlate(n, last):
        s = lax.div(n, REACH + 1)
        k = lax.rem(n, REACH + 1)
        partner = HALO + s - k
        centre = jnp.where(k == 0, HALO + RING + s, partner)
        for tile in range(2):
            for parity in range(2):
                place = n * 4 + tile * 2 + parity
                acc = [[totals[place, q * 3 + m] for m in range(3)] for q in range(8)]
                for w in range(WIDTH):
                    left = [[sources[s, w, m, tile, 8 * i:8 * i + 8, :] for m in range(3)] for i in range(4)]
                    for j in range(-1, 4):
                        at = slice(8 * j + 8, 8 * j + 16)
                        right = [sums[partner, w, parity, m, tile, at, :] for m in range(3)]
                        for i in range(4):
                            q = j - i + 4
                            if not 0 <= q < 8:
                                continue
                            used = right
                            if parity == 0 and q == 4:
                                used = [sums[centre, w, 0, m, tile, at, :] for m in range(3)]
                            for m in range(3):
                                acc[q][m] = acc[q][m] + left[i][m] * used[m]
                if last:
                    where = pl.ds(n * 16 + parity, 8, stride=2)
                    real = fold([a + b for a, b, c in acc])
                    imag = fold([c - a + b for a, b, c in acc])
                    panels[tile, where, :] = real
                    panels[2 + tile, where, :] = imag
                else:
                    for q in range(8):
                        for m in range(3):
                            totals[place, q * 3 + m] = acc[q][m]

    def loop(start, stop, body):
        def step(n, carry):
            body(n)
            return carry

        lax.fori_loop(start, stop, step, 0)

    def one_chunk(chunk, last):
        for source in range(RING - HALO, RING):
            @pl.when(z != source)
            def _():
                block_arrival(chunk, source).wait_recv()

        @pl.when(has_next)
        def _():
            halo_copy(chunk).start()

        for source in range(RING - HALO):
            @pl.when(z != source)
            def _():
                block_arrival(chunk, source).wait_recv()

        for d in order:
            block_copy(chunk, d).wait_send()
        if not last:
            @pl.when(jnp.logical_not(first_sent) & (chunk + AHEAD < CHUNKS))
            def _():
                send_chunk(chunk + AHEAD)

            @pl.when(first_sent & (chunk + AHEAD + EARLY < CHUNKS))
            def _():
                send_chunk(chunk + AHEAD + EARLY)

        loop(HALO, HALO + RING, lambda n: prepare(chunk, n, True))
        loop(REACH * (REACH + 1), RING * (REACH + 1), lambda n: correlate(n, last))

        @pl.when(has_prev)
        def _():
            halo_copy(chunk).wait_recv()

        loop(0, HALO, lambda n: prepare(chunk, n, False))
        loop(0, REACH * (REACH + 1), lambda n: correlate(n, last))

        @pl.when(has_next)
        def _():
            halo_copy(chunk).wait_send()

    loop(0, CHUNKS - 1, lambda chunk: one_chunk(chunk, False))
    one_chunk(CHUNKS - 1, True)

    for d in order:
        bins_copy(d).wait()
    own_bins.wait()
    own_table.wait()

    index = lax.broadcasted_iota(jnp.int32, (128, PANELS), 0)
    owner = lax.rem(index, 2) * (COLS * RING) + lax.rem(lax.div(index, 4), COLS) * RING + lax.div(index, 16)
    bin_ids = BIN_DEV * owner + lax.rem(lax.div(index, 2), 2)
    binned = jnp.zeros((128, 512), F32)
    for s in range(RING):
        hot = jnp.where(bin_ids == bins_in[s], 1.0, 0.0).astype(BF16)
        rows = slice(s * PANELS, (s + 1) * PANELS)
        for part in split_two(jnp.concatenate([panels[t, rows, :] for t in range(4)], axis=1)):
            binned = binned + jnp.dot(hot, part, preferred_element_type=F32)
    high, low = split_two(binned)
    table_high, table_low = split_two(table[...])
    lagged = (
        jnp.dot(high, table_high, preferred_element_type=F32)
        + jnp.dot(low, table_high, preferred_element_type=F32)
        + jnp.dot(high, table_low, preferred_element_type=F32)
    )
    a_out[...] = lagged.reshape(RING, 16, LAGS)

    def a_copy(d):
        to = ring_peer(d)
        return pltpu.make_async_remote_copy(
            src_ref=a_out.at[to], dst_ref=a_in.at[z], send_sem=a_send.at[d], recv_sem=a_recv.at[d],
            device_id=(base + to, seg), device_id_type=MESH,
        )

    def b_copy(d):
        to = y_peer(d)
        return pltpu.make_async_remote_copy(
            src_ref=b_out.at[to], dst_ref=b_in.at[y], send_sem=b_send.at[d], recv_sem=b_recv.at[d],
            device_id=y_device(to), device_id_type=MESH,
        )

    def c_copy(d):
        to = side_peer(d)
        return pltpu.make_async_remote_copy(
            src_ref=c_out.at[to], dst_ref=c_in.at[side], send_sem=c_send.at[d], recv_sem=c_recv.at[d],
            device_id=side_device(to), device_id_type=MESH,
        )

    for d in order:
        a_copy(d).start()
    total = a_out[z]
    for d in order:
        a_copy(d).wait_recv()
    for d in range(1, RING):
        total = total + a_in[ring_peer(d)]
    for r in range(COLS):
        b_out[r] = total[4 * r:4 * r + 4, :]
    for d in range(1, COLS):
        b_copy(d).start()
    total = b_out[y]
    for d in range(1, COLS):
        b_copy(d).wait_recv()
    for d in range(1, COLS):
        total = total + b_in[y_peer(d)]
    for g in range(SEGS):
        both = jnp.concatenate([total[0:2, g * 64:g * 64 + 64], total[2:4, g * 64:g * 64 + 64]], axis=1)
        for r in range(2):
            c_out[r * SEGS + g] = both[r:r + 1, :]
    for d in range(1, SIDES):
        c_copy(d).start()
    result = c_out[side]
    for d in range(1, SIDES):
        c_copy(d).wait_recv()
    for d in range(1, SIDES):
        result = result + c_in[side_peer(d)]
    result = result * norm_factor
    o_ref[0:1, :] = result[:, 0:64]
    o_ref[1:2, :] = result[:, 64:128]
    for d in order:
        a_copy(d).wait_send()
    for d in range(1, COLS):
        b_copy(d).wait_send()
    for d in range(1, SIDES):
        c_copy(d).wait_send()


def on_device(spectra, pair_bins):
    window_count = spectra.shape[1]
    freq_count = spectra.shape[3]
    panel_count = pair_bins.shape[1]
    norm_factor = 1.0 / math.sqrt(
        window_count * SEGS * BLOCK * BIN_WIDTH * freq_count * panel_count / BIN_DEV
    )
    table = jnp.asarray(lag_table(freq_count, LAGS))
    vmem = pl.BlockSpec(memory_space=pltpu.VMEM)
    anywhere = pl.BlockSpec(memory_space=pl.ANY)
    dma = pltpu.SemaphoreType.DMA
    return pl.pallas_call(
        functools.partial(kernel, norm_factor),
        out_shape=jax.ShapeDtypeStruct((BIN_DEV, LAGS // SEGS), F32),
        in_specs=[anywhere, anywhere, anywhere],
        out_specs=vmem,
        scratch_shapes=[
            pltpu.VMEM((HALO + RING, 2, RING, BLOCK, 256), BF16),
            pltpu.VMEM((RING, WIDTH, 3, 2, BLOCK, 128), F32),
            pltpu.VMEM((HALO + 2 * RING, WIDTH, 2, 3, 2, BLOCK + 8, 128), F32),
            pltpu.VMEM((RING * (REACH + 1) * 4, 24, 8, 128), F32),
            pltpu.VMEM((4, RING * PANELS, 128), F32),
            pltpu.VMEM((RING, 1, PANELS), jnp.int32),
            pltpu.VMEM((2 * 256, LAGS), F32),
            pltpu.VMEM((RING, 16, LAGS), F32),
            pltpu.VMEM((RING, 16, LAGS), F32),
            pltpu.VMEM((COLS, 4, LAGS), F32),
            pltpu.VMEM((COLS, 4, LAGS), F32),
            pltpu.VMEM((SIDES, 1, 128), F32),
            pltpu.VMEM((SIDES, 1, 128), F32),
            dma((3,)),
            dma((CHUNKS, RING)), dma((CHUNKS, RING)),
            dma((CHUNKS,)), dma((CHUNKS,)),
            dma((RING,)), dma((RING,)),
            dma((RING,)), dma((RING,)),
            dma((COLS,)), dma((COLS,)),
            dma((SIDES,)), dma((SIDES,)),
        ],
        compiler_params=pltpu.CompilerParams(
            collective_id=0, has_side_effects=True, vmem_limit_bytes=60 * 1024 * 1024
        ),
    )(spectra, pair_bins.transpose(0, 2, 1), table)


def solution(mesh):
    in_specs = (P(None, "seg", "chan", None), P("chan", None, None))
    out_specs = P("chan", "seg")
    return jax.shard_map(
        on_device, mesh=mesh, in_specs=in_specs, out_specs=out_specs, check_vma=False
    )
```

time: 87 us -> 80.5 us (0.925)
  local copies, waits for them, and re-layouts: 3.99 us -> 1.24 us
  Pallas kernels: 81.4 us -> 79.1 us
  other arithmetic: 1.32 us -> 0 us
    unnamed x6 -> x1, local copies, waits for them, and re-layouts: 3.71 us -> 1.24 us
    pallas_call x1, Pallas kernels: 81.4 us -> 79.1 us  [on_device(): pl.pallas_call(functools.partial(kernel, norm_factor), out_shape=jax.Shap...]
    unnamed x1 -> x0, other arithmetic: 1.32 us -> none
where the time goes in v1:
time: 80.5 us; the launch traced here: 80.4 us
  Pallas kernels  79.1 us (98%)
  local copies, waits for them, and re-layouts  1.24 us (2%)
    pallas_call x1, Pallas kernels, on_device(): pl.pallas_call(functools.partial(kernel, norm_factor), out_shape=jax.Shap...  79.1 us

profile of v1, /device:TPU:1, one launch (start us, length us, event | category | flops | bytes accessed | tf_op | source)
XLA Modules:
  0.0 80.4 jit_solution(6616163459701415620)
XLA Ops:
  0.0 79.1 %shard_map.37 = f32[2,64]{1,0:T(2,128)} custom-call(bf16[2,64,32,256]{3,2,1,0:T(8,128)(2,1)} %x_ref.1, s32[1,1,64]{2,1,0:T(1,128)} %bitcast.1, f32[512,256]{1,0:T(8,128)} %constant.2.clone.table_in), custom_call_target="tpu_custom_call" | custom-call | tf_op jit(solution)/shard_map/pallas_call | solution.py:392
  79.1 1.2 %copy.5 = f32[2,64]{1,0:T(2,128)} copy(f32[2,64]{1,0:T(2,128)} %shard_map.37) | data formatting | bytes 1024

commit v2 on v1

--- a/solution.py
+++ b/solution.py
@@ -19,9 +19,11 @@
 MESH = pl.DeviceIdType.MESH
 RING = 8
 ROWS = 8
-COLS = 4
-SEGS = 4
-SIDES = 2 * SEGS
+CORES = 2
+HALVES = 2
+SEGS = HALVES * CORES
+PLANE = ROWS * HALVES
+COLUMN = RING * CORES
 BLOCK = 32
 PANELS = 64
 HALO = REACH
@@ -65,32 +67,33 @@
 
 def kernel(
     norm_factor, x_ref, pb_ref, table_in, o_ref,
-    gathered, sources, sums, totals, panels, bins_in, table, a_out, a_in, b_out, b_in, c_out, c_in,
-    local_sem, x_send, x_recv, h_send, h_recv, p_send, p_recv, a_send, a_recv, b_send, b_recv, c_send, c_recv,
+    gathered, sources, sums, totals, panels, bins_in, table, tables, hot, a_out, a_in, b_out, b_in,
+    local_sem, x_send, x_recv, h_send, h_recv, p_send, p_recv, a_send, a_recv, b_send, b_recv,
 ):
     chan = lax.axis_index("chan")
     seg = lax.axis_index("seg")
     z = lax.rem(chan, RING)
     row = lax.div(chan, RING)
-    y = lax.rem(row, COLS)
-    upper = lax.div(row, COLS)
     base = chan - z
-    side = upper * SEGS + seg
+    half = lax.div(seg, CORES)
+    core = lax.rem(seg, CORES)
+    plane = row * HALVES + half
+    column = z * CORES + core
 
     def ring_peer(d):
         return lax.rem(z + d, RING)
 
-    def y_peer(d):
-        return lax.rem(y + d, COLS)
-
-    def side_peer(d):
-        return lax.rem(side + d, SIDES)
-
-    def side_device(other):
-        return ((lax.div(other, SEGS) * COLS + y) * RING + z, lax.rem(other, SEGS))
-
-    def y_device(other):
-        return ((upper * COLS + other) * RING + z, seg)
+    def plane_peer(d):
+        return lax.rem(plane + d, PLANE)
+
+    def plane_device(other):
+        return (lax.div(other, HALVES) * RING + z, lax.rem(other, HALVES) * CORES + core)
+
+    def column_peer(d):
+        return lax.rem(column + d, COLUMN)
+
+    def column_device(other):
+        return (base + lax.div(other, CORES), half * CORES + lax.rem(other, CORES))
 
     next_row = (lax.rem(row + 1, ROWS) * RING + z, seg)
     prev_row = (lax.rem(row + ROWS - 1, ROWS) * RING + z, seg)
@@ -102,14 +105,12 @@
     def greet(device):
         pl.semaphore_signal(barrier, inc=1, device_id=device, device_id_type=MESH)
 
-    for d in range(1, RING):
-        greet((base + ring_peer(d), seg))
+    for d in range(1, COLUMN):
+        greet(column_device(column_peer(d)))
     greet(next_row)
     greet(prev_row)
-    for d in range(1, COLS):
-        greet(y_device(y_peer(d)))
-    for d in range(1, SIDES):
-        greet(side_device(side_peer(d)))
+    for d in range(1, PLANE):
+        greet(plane_device(plane_peer(d)))
 
     own = pltpu.make_async_copy(x_ref.at[:, pl.ds(z * RING, RING)], gathered.at[HALO + z], local_sem.at[0])
     own.start()
@@ -117,7 +118,7 @@
     own_bins.start()
     own_table = pltpu.make_async_copy(table_in, table, local_sem.at[2])
     own_table.start()
-    pl.semaphore_wait(barrier, RING - 1 + 2 + COLS - 1 + SIDES - 1)
+    pl.semaphore_wait(barrier, COLUMN - 1 + 2 + PLANE - 1)
 
     order = [4, 3, 5, 2, 6, 1, 7]
 
@@ -253,6 +254,20 @@
 
         lax.fori_loop(start, stop, step, 0)
 
+    def inside(i):
+        s = (i >= 1).astype(jnp.int32) + (i >= 3).astype(jnp.int32)
+        return s * (REACH + 1) + i - lax.div(s * (s + 1), 2)
+
+    def across(i):
+        s = (i >= 3).astype(jnp.int32) + (i >= 5).astype(jnp.int32)
+        return s * (REACH + 1) + i + 1 - jnp.where(s == 0, 0, s + 1)
+
+    def sum_bins(part):
+        rows = slice(part * 256, part * 256 + 256)
+        high, low = split_two(jnp.concatenate([panels[t, rows, :] for t in range(4)], axis=1))
+        which = hot[:, rows]
+        return jnp.dot(which, high, preferred_element_type=F32) + jnp.dot(which, low, preferred_element_type=F32)
+
     def one_chunk(chunk, last):
         for source in range(RING - HALO, RING):
             @pl.when(z != source)
@@ -281,20 +296,29 @@
 
         loop(HALO, HALO + RING, lambda n: prepare(chunk, n, True))
         loop(REACH * (REACH + 1), RING * (REACH + 1), lambda n: correlate(n, last))
+        loop(0, 6, lambda i: correlate(inside(i), last))
+        if last:
+            binned = sum_bins(1)
 
         @pl.when(has_prev)
         def _():
             halo_copy(chunk).wait_recv()
 
         loop(0, HALO, lambda n: prepare(chunk, n, False))
-        loop(0, REACH * (REACH + 1), lambda n: correlate(n, last))
+        loop(0, 6, lambda i: correlate(across(i), last))
+        if last:
+            binned = binned + sum_bins(0)
 
         @pl.when(has_next)
         def _():
             halo_copy(chunk).wait_send()
 
-    loop(0, CHUNKS - 1, lambda chunk: one_chunk(chunk, False))
-    one_chunk(CHUNKS - 1, True)
+        return binned if last else None
+
+    def many_chunks(chunk):
+        one_chunk(chunk, False)
+
+    loop(0, CHUNKS - 1, many_chunks)
 
     for d in order:
         bins_copy(d).wait()
@@ -302,80 +326,59 @@
     own_table.wait()
 
     index = lax.broadcasted_iota(jnp.int32, (128, PANELS), 0)
-    owner = lax.rem(index, 2) * (COLS * RING) + lax.rem(lax.div(index, 4), COLS) * RING + lax.div(index, 16)
-    bin_ids = BIN_DEV * owner + lax.rem(lax.div(index, 2), 2)
-    binned = jnp.zeros((128, 512), F32)
-    for s in range(RING):
-        hot = jnp.where(bin_ids == bins_in[s], 1.0, 0.0).astype(BF16)
-        rows = slice(s * PANELS, (s + 1) * PANELS)
-        for part in split_two(jnp.concatenate([panels[t, rows, :] for t in range(4)], axis=1)):
-            binned = binned + jnp.dot(hot, part, preferred_element_type=F32)
+    bin_ids = BIN_DEV * (lax.div(index, 16) * RING + lax.rem(index, 8)) + lax.rem(lax.div(index, 8), 2)
+    for s in range(0, RING, 2):
+        pair = [jnp.where(bin_ids == bins_in[s + i], 1.0, 0.0) for i in range(2)]
+        hot[:, s * PANELS:(s + 2) * PANELS] = jnp.concatenate(pair, axis=1).astype(BF16)
+    tables[0], tables[1] = split_two(table[...])
+
+    binned = one_chunk(CHUNKS - 1, True)
     high, low = split_two(binned)
-    table_high, table_low = split_two(table[...])
-    lagged = (
-        jnp.dot(high, table_high, preferred_element_type=F32)
-        + jnp.dot(low, table_high, preferred_element_type=F32)
-        + jnp.dot(high, table_low, preferred_element_type=F32)
-    )
-    a_out[...] = lagged.reshape(RING, 16, LAGS)
+    both = jnp.dot(jnp.concatenate([high, low], axis=0), tables[0], preferred_element_type=F32)
+    lagged = both[0:128] + both[128:256] + jnp.dot(high, tables[1], preferred_element_type=F32)
+    for h in range(HALVES):
+        a_out[:, h] = lagged[:, h * 128:h * 128 + 128].reshape(ROWS, 16, 128)
 
     def a_copy(d):
-        to = ring_peer(d)
-        return pltpu.make_async_remote_copy(
-            src_ref=a_out.at[to], dst_ref=a_in.at[z], send_sem=a_send.at[d], recv_sem=a_recv.at[d],
-            device_id=(base + to, seg), device_id_type=MESH,
+        to = plane_peer(d)
+        return pltpu.make_async_remote_copy(
+            src_ref=a_out.at[lax.div(to, HALVES), lax.rem(to, HALVES)], dst_ref=a_in.at[plane],
+            send_sem=a_send.at[d], recv_sem=a_recv.at[d],
+            device_id=plane_device(to), device_id_type=MESH,
         )
 
     def b_copy(d):
-        to = y_peer(d)
-        return pltpu.make_async_remote_copy(
-            src_ref=b_out.at[to], dst_ref=b_in.at[y], send_sem=b_send.at[d], recv_sem=b_recv.at[d],
-            device_id=y_device(to), device_id_type=MESH,
-        )
-
-    def c_copy(d):
-        to = side_peer(d)
-        return pltpu.make_async_remote_copy(
-            src_ref=c_out.at[to], dst_ref=c_in.at[side], send_sem=c_send.at[d], recv_sem=c_recv.at[d],
-            device_id=side_device(to), device_id_type=MESH,
-        )
-
-    for d in order:
+        to = column_peer(d)
+        return pltpu.make_async_remote_copy(
+            src_ref=b_out.at[to], dst_ref=b_in.at[column], send_sem=b_send.at[d], recv_sem=b_recv.at[d],
+            device_id=column_device(to), device_id_type=MESH,
+        )
+
+    for d in range(1, PLANE):
         a_copy(d).start()
-    total = a_out[z]
-    for d in order:
+    total = a_out[row, half]
+    for d in range(1, PLANE):
         a_copy(d).wait_recv()
-    for d in range(1, RING):
-        total = total + a_in[ring_peer(d)]
-    for r in range(COLS):
-        b_out[r] = total[4 * r:4 * r + 4, :]
-    for d in range(1, COLS):
+    for d in range(1, PLANE):
+        total = total + a_in[plane_peer(d)]
+    for c in range(CORES):
+        both = jnp.concatenate([total[0:8, c * 64:c * 64 + 64], total[8:16, c * 64:c * 64 + 64]], axis=1)
+        for r in range(RING):
+            b_out[r * CORES + c] = both[r:r + 1, :]
+    for d in range(1, COLUMN):
         b_copy(d).start()
-    total = b_out[y]
-    for d in range(1, COLS):
+    result = b_out[column]
+    for d in range(1, COLUMN):
         b_copy(d).wait_recv()
-    for d in range(1, COLS):
-        total = total + b_in[y_peer(d)]
-    for g in range(SEGS):
-        both = jnp.concatenate([total[0:2, g * 64:g * 64 + 64], total[2:4, g * 64:g * 64 + 64]], axis=1)
-        for r in range(2):
-            c_out[r * SEGS + g] = both[r:r + 1, :]
-    for d in range(1, SIDES):
-        c_copy(d).start()
-    result = c_out[side]
-    for d in range(1, SIDES):
-        c_copy(d).wait_recv()
-    for d in range(1, SIDES):
-        result = result + c_in[side_peer(d)]
+    for d in range(1, COLUMN):
+        result = result + b_in[column_peer(d)]
     result = result * norm_factor
     o_ref[0:1, :] = result[:, 0:64]
     o_ref[1:2, :] = result[:, 64:128]
-    for d in order:
+    for d in range(1, PLANE):
         a_copy(d).wait_send()
-    for d in range(1, COLS):
+    for d in range(1, COLUMN):
         b_copy(d).wait_send()
-    for d in range(1, SIDES):
-        c_copy(d).wait_send()
 
 
 def on_device(spectra, pair_bins):
@@ -402,19 +405,18 @@
             pltpu.VMEM((4, RING * PANELS, 128), F32),
             pltpu.VMEM((RING, 1, PANELS), jnp.int32),
             pltpu.VMEM((2 * 256, LAGS), F32),
-            pltpu.VMEM((RING, 16, LAGS), F32),
-            pltpu.VMEM((RING, 16, LAGS), F32),
-            pltpu.VMEM((COLS, 4, LAGS), F32),
-            pltpu.VMEM((COLS, 4, LAGS), F32),
-            pltpu.VMEM((SIDES, 1, 128), F32),
-            pltpu.VMEM((SIDES, 1, 128), F32),
+            pltpu.VMEM((2, 2 * 256, LAGS), BF16),
+            pltpu.VMEM((128, RING * PANELS), BF16),
+            pltpu.VMEM((ROWS, HALVES, 16, 128), F32),
+            pltpu.VMEM((PLANE, 16, 128), F32),
+            pltpu.VMEM((COLUMN, 1, 128), F32),
+            pltpu.VMEM((COLUMN, 1, 128), F32),
             dma((3,)),
             dma((CHUNKS, RING)), dma((CHUNKS, RING)),
             dma((CHUNKS,)), dma((CHUNKS,)),
             dma((RING,)), dma((RING,)),
-            dma((RING,)), dma((RING,)),
-            dma((COLS,)), dma((COLS,)),
-            dma((SIDES,)), dma((SIDES,)),
+            dma((PLANE,)), dma((PLANE,)),
+            dma((COLUMN,)), dma((COLUMN,)),
         ],
         compiler_params=pltpu.CompilerParams(
             collective_id=0, has_side_effects=True, vmem_limit_bytes=60 * 1024 * 1024

time: 80.5 us -> 77.5 us (0.963)
  Pallas kernels: 79.1 us -> 76.2 us
    pallas_call x1, Pallas kernels: 79.1 us -> 76.2 us  [on_device(): pl.pallas_call(functools.partial(kernel, norm_factor), out_shape=jax.Shap...]
where the time goes in v2:
time: 77.5 us; the launch traced here: 77.4 us
  Pallas kernels  76.2 us (98%)
  local copies, waits for them, and re-layouts  1.24 us (2%)
    pallas_call x1, Pallas kernels, on_device(): pl.pallas_call(functools.partial(kernel, norm_factor), out_shape=jax.Shap...  76.2 us

profile of v2, /device:TPU:1, one launch (start us, length us, event | category | flops | bytes accessed | tf_op | source)
XLA Modules:
  0.0 77.4 jit_solution(12311277938844039372)
XLA Ops:
  0.0 76.2 %shard_map.37 = f32[2,64]{1,0:T(2,128)} custom-call(bf16[2,64,32,256]{3,2,1,0:T(8,128)(2,1)} %x_ref.1, s32[1,1,64]{2,1,0:T(1,128)} %bitcast.1, f32[512,256]{1,0:T(8,128)} %constant.2.clone.table_in), custom_call_target="tpu_custom_call" | custom-call | tf_op jit(solution)/shard_map/pallas_call | solution.py:395
  76.2 1.2 %copy.5 = f32[2,64]{1,0:T(2,128)} copy(f32[2,64]{1,0:T(2,128)} %shard_map.37) | data formatting | bytes 1024

commit v3 on v2

--- a/solution.py
+++ b/solution.py
@@ -30,7 +30,6 @@
 CHUNKS = 8
 WIDTH = RING // CHUNKS
 AHEAD = 2
-EARLY = 1
 F32 = jnp.float32
 BF16 = jnp.bfloat16
 
@@ -46,6 +45,10 @@
 def split_two(value):
     high = value.astype(BF16)
     return high, (value - high.astype(F32)).astype(BF16)
+
+
+def far_first(count):
+    return sorted(range(1, count), key=lambda d: -min(d, count - d))
 
 
 def fold(values):
@@ -105,7 +108,7 @@
     def greet(device):
         pl.semaphore_signal(barrier, inc=1, device_id=device, device_id_type=MESH)
 
-    for d in range(1, COLUMN):
+    for d in far_first(COLUMN):
         greet(column_device(column_peer(d)))
     greet(next_row)
     greet(prev_row)
@@ -139,11 +142,11 @@
             device_id=(base + ring_peer(1), seg), device_id_type=MESH,
         )
 
-    def halo_copy(chunk):
-        return pltpu.make_async_remote_copy(
-            src_ref=gathered.at[pl.ds(RING, HALO), :, pl.ds(chunk * WIDTH, WIDTH)],
-            dst_ref=gathered.at[pl.ds(0, HALO), :, pl.ds(chunk * WIDTH, WIDTH)],
-            send_sem=h_send.at[chunk], recv_sem=h_recv.at[chunk],
+    def halo_copy(chunk, block):
+        return pltpu.make_async_remote_copy(
+            src_ref=gathered.at[RING + block, :, pl.ds(chunk * WIDTH, WIDTH)],
+            dst_ref=gathered.at[block, :, pl.ds(chunk * WIDTH, WIDTH)],
+            send_sem=h_send.at[chunk, block], recv_sem=h_recv.at[chunk, block],
             device_id=next_row, device_id_type=MESH,
         )
 
@@ -158,14 +161,8 @@
         for d in order:
             block_copy(chunk, d).start()
 
-    first_sent = z >= RING - HALO
     for chunk in range(AHEAD):
         send_chunk(chunk)
-
-    @pl.when(first_sent)
-    def _():
-        for chunk in range(AHEAD, AHEAD + EARLY):
-            send_chunk(chunk)
 
     for d in order:
         bins_copy(d).start()
@@ -213,17 +210,15 @@
                     sums[n + RING, w, 0, 1, tile] = other_imag
                     sums[n + RING, w, 0, 2, tile] = other_real + other_imag
 
-    def correlate(n, last):
-        s = lax.div(n, REACH + 1)
-        k = lax.rem(n, REACH + 1)
+    def correlate(s, k, same, last):
+        n = s * (REACH + 1) + k
         partner = HALO + s - k
-        centre = jnp.where(k == 0, HALO + RING + s, partner)
         for tile in range(2):
-            for parity in range(2):
-                place = n * 4 + tile * 2 + parity
-                acc = [[totals[place, q * 3 + m] for m in range(3)] for q in range(8)]
-                for w in range(WIDTH):
-                    left = [[sources[s, w, m, tile, 8 * i:8 * i + 8, :] for m in range(3)] for i in range(4)]
+            for w in range(WIDTH):
+                left = [[sources[s, w, m, tile, 8 * i:8 * i + 8, :] for m in range(3)] for i in range(4)]
+                for parity in range(2):
+                    place = n * 4 + tile * 2 + parity
+                    acc = [[totals[place, q * 3 + m] for m in range(3)] for q in range(8)]
                     for j in range(-1, 4):
                         at = slice(8 * j + 8, 8 * j + 16)
                         right = [sums[partner, w, parity, m, tile, at, :] for m in range(3)]
@@ -232,35 +227,36 @@
                             if not 0 <= q < 8:
                                 continue
                             used = right
-                            if parity == 0 and q == 4:
-                                used = [sums[centre, w, 0, m, tile, at, :] for m in range(3)]
+                            if same and parity == 0 and q == 4:
+                                used = [sums[HALO + RING + s, w, 0, m, tile, at, :] for m in range(3)]
                             for m in range(3):
                                 acc[q][m] = acc[q][m] + left[i][m] * used[m]
-                if last:
-                    where = pl.ds(n * 16 + parity, 8, stride=2)
-                    real = fold([a + b for a, b, c in acc])
-                    imag = fold([c - a + b for a, b, c in acc])
-                    panels[tile, where, :] = real
-                    panels[2 + tile, where, :] = imag
-                else:
-                    for q in range(8):
-                        for m in range(3):
-                            totals[place, q * 3 + m] = acc[q][m]
-
-    def loop(start, stop, body):
+                    if last and w == WIDTH - 1:
+                        where = pl.ds(n * 16 + parity, 8, stride=2)
+                        panels[tile, where, :] = fold([a + b for a, b, c in acc])
+                        panels[2 + tile, where, :] = fold([c - a + b for a, b, c in acc])
+                    else:
+                        for q in range(8):
+                            for m in range(3):
+                                totals[place, q * 3 + m] = acc[q][m]
+
+    def loop(start, stop, body, unroll=1):
         def step(n, carry):
             body(n)
             return carry
 
-        lax.fori_loop(start, stop, step, 0)
-
-    def inside(i):
-        s = (i >= 1).astype(jnp.int32) + (i >= 3).astype(jnp.int32)
-        return s * (REACH + 1) + i - lax.div(s * (s + 1), 2)
+        lax.fori_loop(start, stop, step, 0, unroll=unroll)
+
+    def earlier(i):
+        s = jnp.where(i == 0, 1, 2)
+        return s, jnp.where(i == 2, 2, 1)
 
     def across(i):
         s = (i >= 3).astype(jnp.int32) + (i >= 5).astype(jnp.int32)
-        return s * (REACH + 1) + i + 1 - jnp.where(s == 0, 0, s + 1)
+        return s, i + 1 - jnp.where(s == 0, 0, s + 1)
+
+    def later(i):
+        return HALO + lax.div(i, REACH), 1 + lax.rem(i, REACH)
 
     def sum_bins(part):
         rows = slice(part * 256, part * 256 + 256)
@@ -268,50 +264,65 @@
         which = hot[:, rows]
         return jnp.dot(which, high, preferred_element_type=F32) + jnp.dot(which, low, preferred_element_type=F32)
 
-    def one_chunk(chunk, last):
-        for source in range(RING - HALO, RING):
-            @pl.when(z != source)
-            def _():
-                block_arrival(chunk, source).wait_recv()
-
+    def sent(chunk):
+        for d in order:
+            block_copy(chunk, d).wait_send()
+
+    def halo_sent(chunk):
         @pl.when(has_next)
         def _():
-            halo_copy(chunk).start()
+            for block in range(HALO):
+                halo_copy(chunk, block).wait_send()
+
+    def forward(chunk):
+        for block in range(HALO):
+            @pl.when(z != RING - HALO + block)
+            def _():
+                block_arrival(chunk, RING - HALO + block).wait_recv()
+
+            @pl.when(has_next)
+            def _():
+                halo_copy(chunk, block).start()
+
+    def one_chunk(chunk, last):
+        if not last:
+            forward(chunk)
 
         for source in range(RING - HALO):
             @pl.when(z != source)
             def _():
                 block_arrival(chunk, source).wait_recv()
 
-        for d in order:
-            block_copy(chunk, d).wait_send()
         if not last:
-            @pl.when(jnp.logical_not(first_sent) & (chunk + AHEAD < CHUNKS))
+            sent(chunk)
+
+            @pl.when(chunk + AHEAD < CHUNKS)
             def _():
                 send_chunk(chunk + AHEAD)
 
-            @pl.when(first_sent & (chunk + AHEAD + EARLY < CHUNKS))
-            def _():
-                send_chunk(chunk + AHEAD + EARLY)
-
-        loop(HALO, HALO + RING, lambda n: prepare(chunk, n, True))
-        loop(REACH * (REACH + 1), RING * (REACH + 1), lambda n: correlate(n, last))
-        loop(0, 6, lambda i: correlate(inside(i), last))
+        loop(HALO, HALO + RING, lambda n: prepare(chunk, n, True), 4)
+        loop(0, RING, lambda s: correlate(s, 0, True, last), 4)
+        loop(0, 15, lambda i: correlate(*later(i), False, last), 5)
         if last:
             binned = sum_bins(1)
+        else:
+            @pl.when(chunk == CHUNKS - 2)
+            def _():
+                forward(CHUNKS - 1)
+
+        loop(0, 3, lambda i: correlate(*earlier(i), False, last), 3)
 
         @pl.when(has_prev)
         def _():
-            halo_copy(chunk).wait_recv()
-
-        loop(0, HALO, lambda n: prepare(chunk, n, False))
-        loop(0, 6, lambda i: correlate(across(i), last))
+            for block in range(HALO):
+                halo_copy(chunk, block).wait_recv()
+
+        loop(0, HALO, lambda n: prepare(chunk, n, False), 3)
+        loop(0, 6, lambda i: correlate(*across(i), False, last), 3)
         if last:
             binned = binned + sum_bins(0)
-
-        @pl.when(has_next)
-        def _():
-            halo_copy(chunk).wait_send()
+        else:
+            halo_sent(chunk)
 
         return binned if last else None
 
@@ -365,7 +376,7 @@
         both = jnp.concatenate([total[0:8, c * 64:c * 64 + 64], total[8:16, c * 64:c * 64 + 64]], axis=1)
         for r in range(RING):
             b_out[r * CORES + c] = both[r:r + 1, :]
-    for d in range(1, COLUMN):
+    for d in far_first(COLUMN):
         b_copy(d).start()
     result = b_out[column]
     for d in range(1, COLUMN):
@@ -375,6 +386,8 @@
     result = result * norm_factor
     o_ref[0:1, :] = result[:, 0:64]
     o_ref[1:2, :] = result[:, 64:128]
+    sent(CHUNKS - 1)
+    halo_sent(CHUNKS - 1)
     for d in range(1, PLANE):
         a_copy(d).wait_send()
     for d in range(1, COLUMN):
@@ -413,7 +426,7 @@
             pltpu.VMEM((COLUMN, 1, 128), F32),
             dma((3,)),
             dma((CHUNKS, RING)), dma((CHUNKS, RING)),
-            dma((CHUNKS,)), dma((CHUNKS,)),
+            dma((CHUNKS, HALO)), dma((CHUNKS, HALO)),
             dma((RING,)), dma((RING,)),
             dma((PLANE,)), dma((PLANE,)),
             dma((COLUMN,)), dma((COLUMN,)),

time: 77.5 us -> 76.9 us (level)
  no operation moved by 1% of the time
where the time goes in v3:
time: 76.9 us; the launch traced here: 76.8 us
  Pallas kernels  75.5 us (98%)
  local copies, waits for them, and re-layouts  1.24 us (2%)
    pallas_call x1, Pallas kernels, on_device(): pl.pallas_call(functools.partial(kernel, norm_factor), out_shape=jax.Shap...  75.5 us

profile of v3, /device:TPU:1, one launch (start us, length us, event | category | flops | bytes accessed | tf_op | source)
XLA Modules:
  0.0 76.8 jit_solution(12591362191845570221)
XLA Ops:
  0.0 75.5 %shard_map.37 = f32[2,64]{1,0:T(2,128)} custom-call(bf16[2,64,32,256]{3,2,1,0:T(8,128)(2,1)} %x_ref.1, s32[1,1,64]{2,1,0:T(1,128)} %bitcast.1, f32[512,256]{1,0:T(8,128)} %constant.2.clone.table_in), custom_call_target="tpu_custom_call" | custom-call | tf_op jit(solution)/shard_map/pallas_call | solution.py:408
  75.5 1.2 %copy.5 = f32[2,64]{1,0:T(2,128)} copy(f32[2,64]{1,0:T(2,128)} %shard_map.37) | data formatting | bytes 1024

commit v4 on v3

--- a/solution.py
+++ b/solution.py
@@ -29,7 +29,7 @@
 HALO = REACH
 CHUNKS = 8
 WIDTH = RING // CHUNKS
-AHEAD = 2
+AHEAD = 3
 F32 = jnp.float32
 BF16 = jnp.bfloat16
 

time: 76.9 us -> 76.9 us (level)
  no operation moved by 1% of the time
where the time goes in v4:
time: 76.9 us; the launch traced here: 76.8 us
  Pallas kernels  75.5 us (98%)
  local copies, waits for them, and re-layouts  1.24 us (2%)
    pallas_call x1, Pallas kernels, on_device(): pl.pallas_call(functools.partial(kernel, norm_factor), out_shape=jax.Shap...  75.5 us

profile of v4, /device:TPU:1, one launch (start us, length us, event | category | flops | bytes accessed | tf_op | source)
XLA Modules:
  0.0 76.8 jit_solution(9069136386446947078)
XLA Ops:
  0.0 75.5 %shard_map.37 = f32[2,64]{1,0:T(2,128)} custom-call(bf16[2,64,32,256]{3,2,1,0:T(8,128)(2,1)} %x_ref.1, s32[1,1,64]{2,1,0:T(1,128)} %bitcast.1, f32[512,256]{1,0:T(8,128)} %constant.2.clone.table_in), custom_call_target="tpu_custom_call" | custom-call | tf_op jit(solution)/shard_map/pallas_call | solution.py:408
  75.5 1.2 %copy.5 = f32[2,64]{1,0:T(2,128)} copy(f32[2,64]{1,0:T(2,128)} %shard_map.37) | data formatting | bytes 1024
